TPU v7x, 32 devices: a whole 2x2x4 slice. The times are simulated.
32 devices in a mesh: rot: 4 (over y, core), tile: 8 (over z, x).
Axes of the slice: x: 2, y: 2, z: 4, core: 2. Of those that a mesh axis runs over, the one named last changes fastest.
Arguments:
- volume: float32 [8, 32, 32, 128], P('tile')
- templates: bfloat16 [32, 64000], replicated
- rot_ids: int32 [4], P('rot'), may hold values from 0 to 31
Outputs:
- soft_map: float32 [8, 32, 32, 128], P('tile', 'rot')
All inputs are finite; a program needn't handle non-finite values.
Results may differ from a plain program's by a relative error of at most 0.0003.
Values sent between devices are 32-bit elements; how exact they have to be, the bound alone decides.
A program may use at most 128 MiB of HBM per device.

v0:
```python
import functools
import math

import jax
import jax.numpy as jnp
import ml_dtypes
import numpy as np
from jax import lax
from jax.experimental import pallas as pl
from jax.experimental.pallas import tpu as pltpu
from jax.sharding import PartitionSpec as P

TMPL = 40
HALF = TMPL // 2
VAR_FLOOR = 0.05
EPSILON = 1e-06
SHARPNESS = 2.0
LANES = 128
VMEM = 56 * 1024 * 1024


def sphere():
    offsets = np.arange(TMPL) - (TMPL - 1) / 2.0
    squares = offsets**2
    radius_sq = squares[:, None, None] + squares[None, :, None] + squares[None, None, :]
    return (radius_sq <= (TMPL / 2.0) ** 2).astype(np.float64)


def halves(table):
    high = table.astype(ml_dtypes.bfloat16)
    low = (table - high.astype(np.float64)).astype(ml_dtypes.bfloat16)
    return high, low


def left_table(table):
    high, low = halves(table)
    return np.concatenate([high, high, low], axis=1)


def right_table(table):
    high, low = halves(table)
    return np.concatenate([high, high, low], axis=0)


def wide(table, axis, size):
    pad = [(0, 0), (0, 0)]
    pad[axis] = (0, size - table.shape[axis])
    return np.pad(table, pad)


def angles(length, rows, columns):
    return 2.0 * math.pi * ((np.asarray(rows)[:, None] * np.asarray(columns)[None, :]) % length) / length


def y_forward(length, inputs):
    theta = angles(length, np.arange(length), np.arange(length))[:, : min(inputs, length)]
    return left_table(np.concatenate([wide(np.cos(theta), 1, inputs), wide(np.sin(theta), 1, inputs)], axis=0))


def z_forward(length, inputs, freqs):
    theta = angles(length, np.arange(inputs), np.arange(freqs))
    return right_table(np.concatenate([wide(np.cos(theta), 1, LANES), wide(np.sin(theta), 1, LANES)], axis=1))


def y_inverse(length, padded, outputs):
    theta = angles(length, np.arange(outputs), np.arange(length))
    both = np.concatenate([np.cos(theta), np.sin(theta)], axis=0) / length
    return left_table(wide(both, 1, padded))


def z_inverse(length, outputs, freqs, extra):
    theta = angles(length, np.arange(freqs), np.arange(outputs) - HALF)
    index = np.arange(freqs)
    weight = np.where((index == 0) | (2 * index == length), 1.0, 2.0)[:, None] / (length * extra)
    real = wide(np.cos(theta) * weight, 0, LANES)
    imag = wide(-np.sin(theta) * weight, 0, LANES)
    return right_table(np.concatenate([real, imag], axis=0))


def mask_spectrum(places, length_x, length_y, length_z, freqs):
    field = np.zeros((length_x, length_y, length_z))
    field[np.asarray(places), :TMPL, :TMPL] = sphere()
    spec = np.fft.rfftn(field)
    gap = ((0, 0), (0, 0), (0, LANES - freqs))
    return np.concatenate([np.pad(spec.real, gap), np.pad(spec.imag, gap)], axis=2).astype(np.float32)


def plus(a, b):
    if a is None:
        return b
    if b is None:
        return a
    return (a[0] + b[0], a[1] + b[1])


def minus(a, b):
    if b is None:
        return a
    if a is None:
        return (-b[0], -b[1])
    return (a[0] - b[0], a[1] - b[1])


def turn(a, step, length):
    if a is None:
        return None
    step %= length
    re, im = a
    eighth = 8 * step
    if eighth % length == 0:
        part = eighth // length
        root = math.sqrt(0.5)
        if part == 0:
            return a
        if part == 2:
            return (-im, re)
        if part == 4:
            return (-re, -im)
        if part == 6:
            return (im, -re)
        if part == 1:
            return ((re - im) * root, (re + im) * root)
        if part == 3:
            return ((re + im) * -root, (re - im) * root)
        if part == 5:
            return ((im - re) * root, (re + im) * -root)
        return ((re + im) * root, (im - re) * root)
    c = math.cos(2.0 * math.pi * step / length)
    s = math.sin(2.0 * math.pi * step / length)
    return (re * c - im * s, re * s + im * c)


def small_dft(values, sign):
    length = len(values)
    if length == 1:
        return values
    if length % 2 == 0:
        even = small_dft(values[0::2], sign)
        odd = small_dft(values[1::2], sign)
        odd = [turn(value, sign * k, length) for k, value in enumerate(odd)]
        return [plus(e, o) for e, o in zip(even, odd)] + [minus(e, o) for e, o in zip(even, odd)]
    sums = []
    for k in range(length):
        total = None
        for n in range(length):
            total = plus(total, turn(values[n], sign * n * k, length))
        sums.append(total)
    return sums


def pieces(values, axis):
    high = values.astype(jnp.bfloat16)
    low = (values - high.astype(jnp.float32)).astype(jnp.bfloat16)
    return jnp.concatenate([high, low, high], axis=axis)


def dot(a, b):
    return jnp.dot(a, b, preferred_element_type=jnp.float32)


def planes(pair, ly, tz, length_y):
    o = dot(ly, pieces(pair, 0))
    g = jnp.concatenate([o[:, :LANES], o[:, LANES:]], axis=0)
    h = dot(pieces(g, 1), tz)
    outs = []
    for which in range(2):
        base = 2 * length_y * which
        c = h[base : base + length_y]
        s = h[base + length_y : base + 2 * length_y]
        outs.append((c[:, :LANES] - s[:, LANES:], -s[:, :LANES] - c[:, LANES:]))
    return outs


def template_kernel(length_y, grid_ref, ly_ref, tz_ref, out_ref):
    def step(pair, carry):
        both = jnp.concatenate([grid_ref[2 * pair], grid_ref[2 * pair + 1]], axis=1)
        outs = planes(both, ly_ref[...], tz_ref[...], length_y)
        for which, (re, im) in enumerate(outs):
            out_ref[2 * pair + which, :, :LANES] = re
            out_ref[2 * pair + which, :, LANES:] = im
        return carry

    lax.fori_loop(0, TMPL // 2, step, 0, unroll=2)


def main_kernel(
    dims, places, voxels,
    ext_ref, khat_ref, mhat_hbm, phase_ref, ly_ref, tz_ref, iy_ref, iz_ref,
    score_ref, scale_ref,
    fields, mhat, stage, mixed, rows, local, sem,
):
    size_in, length_y, padded, size_x, size_y, inner, outer = dims
    length_x = inner * outer
    fetch = pltpu.make_async_copy(mhat_hbm, mhat, sem)
    fetch.start()

    def forward(x, carry):
        v = ext_ref[x]
        outs = planes(jnp.concatenate([v, v * v], axis=1), ly_ref[...], tz_ref[...], length_y)
        for which, (re, im) in enumerate(outs):
            fields[which, x, :, :LANES] = re
            fields[which, x, :, LANES:] = im
        return carry

    lax.fori_loop(0, size_in, forward, 0, unroll=2)
    rows[:, length_y:, :] = jnp.zeros((rows.shape[0], padded - length_y, 2 * LANES), jnp.float32)
    fetch.wait()

    def block(r, carry):
        at = pl.ds(pl.multiple_of(r * 8, 8), 8)

        def first(read, slot):
            for n2 in range(inner):
                values = [read(inner * n1 + n2) for n1 in range(outer)]
                for k1, value in enumerate(small_dft(values, -1)):
                    re, im = turn(value, -n2 * k1, length_x)
                    stage[slot, k1 * inner + n2, :, :LANES] = re
                    stage[slot, k1 * inner + n2, :, LANES:] = im

        def field_reader(which):
            def read(n):
                if n >= size_in:
                    return None
                return (fields[which, n, at, :LANES], fields[which, n, at, LANES:])

            return read

        def kernel_reader(n):
            if n not in places:
                return None
            q = places.index(n)
            return (khat_ref[q, at, :LANES], khat_ref[q, at, LANES:])

        first(field_reader(0), 0)
        first(field_reader(1), 1)
        first(kernel_reader, 2)

        def second(slot, k1):
            values = [
                (stage[slot, k1 * inner + n2, :, :LANES], stage[slot, k1 * inner + n2, :, LANES:])
                for n2 in range(inner)
            ]
            return small_dft(values, -1)

        def times(a, b):
            return (a[0] * b[0] + a[1] * b[1], a[1] * b[0] - a[0] * b[1])

        for k1 in range(outer):
            volume = second(0, k1)
            template = second(2, k1)
            mask = [
                (mhat[k1 + outer * k2, at, :LANES], mhat[k1 + outer * k2, at, LANES:])
                for k2 in range(inner)
            ]
            square = second(1, k1)
            products = (
                [times(a, b) for a, b in zip(volume, template)],
                [times(a, b) for a, b in zip(volume, mask)],
                [times(a, b) for a, b in zip(square, mask)],
            )
            for slot, product in enumerate(products):
                for n2, value in enumerate(small_dft(product, 1)):
                    re, im = turn(value, n2 * k1, length_x)
                    mixed[slot, k1 * inner + n2, :, :LANES] = re
                    mixed[slot, k1 * inner + n2, :, LANES:] = im

        for n2 in range(inner):
            def load(slot):
                return [
                    (mixed[slot, k1 * inner + n2, :, :LANES], mixed[slot, k1 * inner + n2, :, LANES:])
                    for k1 in range(outer)
                ]

            sums = small_dft(load(0), 1)
            for n1 in range(size_x // inner):
                rows[inner * n1 + n2, at, :LANES] = sums[n1][0]
                rows[inner * n1 + n2, at, LANES:] = sums[n1][1]
            for slot in (1, 2):
                re_sum = None
                for k1, (re, im) in enumerate(load(slot)):
                    c, s = phase_ref[k1, 0], phase_ref[k1, 1]
                    re_part, im_part = re * c - im * s, re * s + im * c
                    if re_sum is None:
                        re_sum, im_sum = re_part, im_part
                    else:
                        re_sum, im_sum = re_sum + re_part, im_sum + im_part
                target = size_x + (slot - 1) * inner + n2
                rows[target, at, :LANES] = re_sum
                rows[target, at, LANES:] = im_sum
        return carry

    lax.fori_loop(0, length_y // 8, block, 0)

    group = 4

    def inverse(step, carry):
        flat = []
        for i in range(group):
            o = dot(iy_ref[...], pieces(rows[step * group + i], 0))
            c, s = o[:size_y], o[size_y:]
            re = c[:, :LANES] - s[:, LANES:]
            im = c[:, LANES:] + s[:, :LANES]
            flat.append(jnp.concatenate([re, im], axis=1))
        result = dot(pieces(jnp.concatenate(flat, axis=0), 1), iz_ref[...])
        for i in range(group):
            local[step * group + i] = result[i * size_y : (i + 1) * size_y]
        return carry

    lax.fori_loop(0, (size_x + 2 * inner) // group, inverse, 0)
    score_ref[...] = local[:size_x]
    mean = local[size_x : size_x + inner] / voxels
    square = local[size_x + inner :] / voxels
    std = jnp.sqrt(jnp.maximum(square - mean * mean, VAR_FLOOR))
    scale_ref[...] = SHARPNESS / (math.sqrt(voxels) * std)


def normalize(flat_grid, sphere_mask, voxel_count):
    template = flat_grid.astype(jnp.float32).reshape(TMPL, TMPL, TMPL)
    centre = jnp.sum(template * sphere_mask) / voxel_count
    centred = (template - centre) * sphere_mask
    spread = jnp.sqrt(jnp.sum(centred * centred) / voxel_count + EPSILON)
    return centred / spread


def halo(block, distance, across, axis):
    tiles = lax.axis_size("tile")
    stays = lambda t: distance > 1 or t % across != 0
    up = [(t - distance, t) for t in range(distance, tiles) if distance >= across or t % across != 0]
    down = [(t, s) for s, t in up]
    size = block.shape[axis]
    lower = lax.ppermute(lax.slice_in_dim(block, size - HALF, size, axis=axis), "tile", up)
    upper = lax.ppermute(lax.slice_in_dim(block, 0, HALF, axis=axis), "tile", down)
    return lower, upper


def shards(volume, templates, rot_ids):
    tile_count = lax.axis_size("tile")
    rots = lax.axis_size("rot")
    across = min(tile_count, 8)
    down = tile_count // across
    block = volume[0]
    size_x, size_y, size_z = block.shape
    inner = size_x // rots
    if down > 1:
        lower, upper = halo(block, across, across, 0)
        block = jnp.concatenate([lower, block, upper], axis=0)
        length_x = size_x + TMPL
        places = tuple(range(TMPL))
    else:
        length_x = -(-(size_x + HALF) // (2 * inner)) * 2 * inner
        places = tuple((q - HALF) % length_x for q in range(TMPL))
    outer = length_x // inner
    size_in = block.shape[0]
    length_y = size_y + TMPL
    padded = -(-length_y // 16) * 16
    length_z = size_z + HALF
    freqs = length_z // 2 + 1

    mask = sphere()
    voxels = float(mask.sum())
    if across > 1:
        lower, upper = halo(block, 1, across, 1)
    else:
        lower = upper = jnp.zeros((size_in, HALF, size_z), jnp.float32)
    bottom = jnp.zeros((size_in, padded - length_y, size_z), jnp.float32)
    extended = jnp.concatenate([lower, block, upper, bottom], axis=1)

    tz = jnp.asarray(z_forward(length_z, LANES, freqs))
    kernel = normalize(templates[rot_ids[0]], jnp.asarray(mask, jnp.float32), voxels)
    kernel_rows = 48
    kernel = jnp.pad(kernel, ((0, 0), (0, kernel_rows - TMPL), (0, LANES - TMPL)))
    vmem = pl.BlockSpec(memory_space=pltpu.VMEM)
    khat = pl.pallas_call(
        functools.partial(template_kernel, length_y),
        out_shape=jax.ShapeDtypeStruct((TMPL, length_y, 2 * LANES), jnp.float32),
        in_specs=[vmem] * 3,
        out_specs=vmem,
        compiler_params=pltpu.CompilerParams(vmem_limit_bytes=VMEM),
        cost_estimate=pl.CostEstimate(flops=4 * 10**9, bytes_accessed=4 * 10**6, transcendentals=0),
        name="template_spectrum",
    )(kernel, jnp.asarray(y_forward(length_y, kernel_rows)), tz)

    mhat = jnp.asarray(mask_spectrum(places, length_x, length_y, length_z, freqs))
    angle = (jnp.arange(outer) * lax.axis_index("rot") % outer).astype(jnp.float32) * (2.0 * math.pi / outer)
    phase = jnp.stack([jnp.cos(angle), jnp.sin(angle)], axis=1)
    dims = (size_in, length_y, padded, size_x, size_y, inner, outer)
    scores, scale = pl.pallas_call(
        functools.partial(main_kernel, dims, places, voxels),
        out_shape=(
            jax.ShapeDtypeStruct((size_x, size_y, size_z), jnp.float32),
            jax.ShapeDtypeStruct((inner, size_y, size_z), jnp.float32),
        ),
        in_specs=[
            vmem, vmem, pl.BlockSpec(memory_space=pl.ANY), pl.BlockSpec(memory_space=pltpu.SMEM),
            vmem, vmem, vmem, vmem,
        ],
        out_specs=(vmem, vmem),
        scratch_shapes=[
            pltpu.VMEM((2, size_in, length_y, 2 * LANES), jnp.float32),
            pltpu.VMEM((length_x, length_y, 2 * LANES), jnp.float32),
            pltpu.VMEM((3, length_x, 8, 2 * LANES), jnp.float32),
            pltpu.VMEM((3, length_x, 8, 2 * LANES), jnp.float32),
            pltpu.VMEM((size_x + 2 * inner, padded, 2 * LANES), jnp.float32),
            pltpu.VMEM((size_x + 2 * inner, size_y, size_z), jnp.float32),
            pltpu.SemaphoreType.DMA,
        ],
        compiler_params=pltpu.CompilerParams(vmem_limit_bytes=VMEM),
        name="correlate",
    )(
        extended, khat, mhat, phase,
        jnp.asarray(y_forward(length_y, padded)), tz,
        jnp.asarray(y_inverse(length_y, padded, size_y)),
        jnp.asarray(z_inverse(length_z, size_z, freqs, length_x)),
    )
    gathered = lax.all_to_all(scores, "rot", split_axis=0, concat_axis=0, tiled=True)
    gathered = gathered.reshape(rots, inner, size_y, size_z) * scale[None]
    largest = jnp.max(gathered, axis=0)
    return (largest + jnp.log(jnp.sum(jnp.exp(gathered - largest[None]), axis=0)))[None]


def solution(mesh):
    return jax.shard_map(
        shards,
        mesh=mesh,
        in_specs=(P("tile", None, None, None), P(), P("rot")),
        out_specs=P("tile", "rot", None, None),
        check_vma=False,
    )
```

profile of v0, /device:TPU:9, one launch (start us, length us, event | category | flops | bytes accessed | tf_op | source)
XLA Modules:
  0.0 67.4 jit_solution(8325233104835935328)
XLA Ops:
  0.0 0.0 copy-start.1
  0.0 1.2 %fusion.5 = (f32[32,20,128]{2,1,0:T(8,128)S(1)}, f32[32,20,128]{2,1,0:T(8,128)S(1)}) fusion(f32[32,32,128]{2,1,0:T(8,128)} %bitcast.10), kind=kLoop, calls=%fused_computation.17 | loop fusion | bytes 1310720 | tf_op jit(solution)/shard_map/slice | solution.py:331
  1.2 3.1 %collective-permute-start = (f32[32,20,128]{2,1,0:T(8,128)S(1)}, f32[32,20,128]{2,1,0:T(8,128)S(1)}, u32[]{:S(2)}, u32[]{:S(2)}) collective-permute-start(f32[32,20,128]{2,1,0:T(8,128)S(1)} %get-tuple-element.9), channel_id=1, source_target_pairs={{0,1},{1,2},{2,3},{3,4},{4,5},{5,6},{6,7},{8,9},{9,10},{10,11},{11... | collective-permute-start | bytes 983048 | tf_op jit(solution)/shard_map/ppermute | solution.py:331
  4.4 3.1 %collective-permute-start.1 = (f32[32,20,128]{2,1,0:T(8,128)S(1)}, f32[32,20,128]{2,1,0:T(8,128)S(1)}, u32[]{:S(2)}, u32[]{:S(2)}) collective-permute-start(f32[32,20,128]{2,1,0:T(8,128)S(1)} %get-tuple-element.10), channel_id=1, source_target_pairs={{1,0},{2,1},{3,2},{4,3},{5,4},{6,5},{7,6},{9,8},{10,9},{11,10},{12... | collective-permute-start | bytes 983048 | tf_op jit(solution)/shard_map/ppermute | solution.py:332
  8.1 0.0 copy-done.1
  8.1 2.4 %multiply_reduce_fusion.2 = f32[]{:T(128)} fusion(f32[1,64000]{1,0:T(1,128)S(1)} %copy-done.1, bf16[32,64000]{1,0:T(8,128)(2,1)} %param.11, s32[]{:T(128)S(6)} %select_n.21), kind=kLoop, calls=%fused_computation.5 | loop fusion | flops 191999 | bytes 384008 | tf_op jit(solution)/shard_map/reduce_sum | solution.py:319
  11.1 2.4 %multiply_reduce_fusion.1 = f32[]{:T(128)} fusion(f32[1,64000]{1,0:T(1,128)S(1)} %copy-done.1, f32[]{:T(128)S(6)} %div.12, bf16[32,64000]{1,0:T(8,128)(2,1)} %param.11, s32[]{:T(128)S(6)} %select_n.21), kind=kLoop, calls=%fused_computation.4 | loop fusion | flops 319999 | bytes 384012 | tf_op jit(solution)/shard_map/reduce_sum | solution.py:321
  14.1 2.2 %divide_reduce_fusion = f32[64000]{0:T(1024)S(1)} fusion(f32[1,64000]{1,0:T(1,128)S(1)} %copy-done.1, f32[]{:T(128)S(6)} %sqrt.3, f32[]{:T(128)S(6)} %div.12, bf16[32,64000]{1,0:T(8,128)(2,1)} %param.11, s32[]{:T(128)S(6)} %select_n.21), kind=kLoop, calls=%fused_computation.3 | loop fusion | flops 256000 | bytes 640012 | tf_op jit(solution)/shard_map/div | solution.py:322
  16.4 0.6 reshape.88
  16.9 0.1 fusion.3
  17.0 0.7 %copy.11.phase_ref = f32[8,2]{1,0:T(8,128)} copy(f32[8,2]{0,1:T(2,128)S(1)} %pad_maximum_fusion) | data formatting | bytes 128 | tf_op jit(solution)/shard_map/stack | solution.py:385
  17.7 1.0 %pad.4.grid_ref = f32[40,48,128]{2,1,0:T(8,128)} pad(f32[40,40,40]{2,1,0:T(8,128)S(1)} %reshape.88, f32[]{:T(128)} %constant.20.clone.1), padding=0_0x0_8x0_88 | pad | bytes 1239044 | tf_op jit(solution)/shard_map/jit(_pad)/pad | solution.py:371
  18.7 0.1 pad.10.clone
  18.8 0.0 copy-start
  18.8 7.3 %template_spectrum.1.khat_ref = f32[40,72,256]{2,1,0:T(8,128)} custom-call(f32[40,48,128]{2,1,0:T(8,128)} %pad.4.grid_ref, bf16[144,144]{1,0:T(8,128)(2,1)} %constant.53.clone.ly_ref, bf16[384,256]{1,0:T(8,128)(2,1)} %constant.51.clone.tz_ref), custom_call_target="tpu_custom_call" | custom-call | flops 4000000000 | bytes 4000000 | tf_op jit(solution)/shard_map/template_spectrum/pallas_call | solution.py:373
  26.1 0.0 collective-permute-done
  26.1 0.0 collective-permute-done.1
  26.1 0.0 copy-done
  26.1 1.3 %maximum_maximum_fusion.ext_ref = f32[32,80,128]{2,1,0:T(8,128)} fusion(f32[32,20,128]{2,1,0:T(8,128)S(1)} %collective-permute-done.1, f32[32,32,128]{2,1,0:T(8,128)S(1)} %bitcast.11, f32[32,20,128]{2,1,0:T(8,128)S(1)} %collective-permute-done, f32[80]{0:T(128)S(1)} %pad.10.clone), kind=kLoop, calls=%fused_computation | loop fusion | flops 983040 | bytes 2490688 | tf_op jit(solution)/shard_map/concatenate | solution.py:366
  27.3 25.6 %correlate.1 = (f32[32,32,128]{2,1,0:T(8,128)}, f32[8,32,128]{2,1,0:T(8,128)}) custom-call(f32[32,80,128]{2,1,0:T(8,128)} %maximum_maximum_fusion.ext_ref, f32[40,72,256]{2,1,0:T(8,128)} %template_spectrum.1.khat_ref, f32[64,72,256]{2,1,0:T(8,128)} %constant.54.clone.mhat_hbm, f32[8,2]{1,0:T(8,128)} %copy.11.phase_ref, ...), custom_call_target="tpu_custom_call" | custom-call | tf_op jit(solution)/shard_map/correlate/pallas_call | solution.py:387
  53.0 0.0 copy-start.2
  53.0 12.6 %all_to_all.5 = f32[32,32,128]{2,1,0:T(8,128)S(1)} all-to-all(f32[32,32,128]{2,1,0:T(8,128)} %get-tuple-element.7), channel_id=1, replica_groups=mesh['rot'=4,'tile'=8] {'rot'}, dimensions={0} | all-to-all | bytes 1048576 | tf_op jit(solution)/shard_map/all_to_all | solution.py:415
  65.6 1.0 %multiply_reduce_fusion = f32[8,32,128]{2,1,0:T(8,128)S(1)} fusion(f32[4,8,32,128]{3,2,1,0:T(8,128)S(1)} %bitcast.8, f32[8,32,128]{2,1,0:T(8,128)} %get-tuple-element.8), kind=kLoop, calls=%fused_computation.2 | loop fusion | flops 229376 | bytes 786432 | tf_op jit(solution)/shard_map/reduce_max | solution.py:417
  66.6 0.0 copy-done.2
  66.6 0.1 exponential_reduce_fusion
  66.7 0.7 %add_bitcast_fusion = f32[1,8,32,128]{3,2,1,0:T(8,128)} fusion(f32[8,32,128]{2,1,0:T(8,128)S(1)} %multiply_reduce_fusion, f32[8,32,128]{2,1,0:T(8,128)S(1)} %exponential_reduce_fusion), kind=kLoop, calls=%fused_computation.7 | loop fusion | flops 32768 | bytes 393216 | tf_op jit(solution)/shard_map/add | solution.py:418
  (2 shorter events, 0.0 us)
Async XLA Ops:
  0.0 8.1 %copy-start.1 = (f32[1,64000]{1,0:T(1,128)S(1)}, f32[1,64000]{1,0:T(1,128)}, u32[]{:S(2)}) copy-start(f32[1,64000]{1,0:T(1,128)} %constant.63) | copy-start | bytes 768004
  1.2 24.8 %collective-permute-start = (f32[32,20,128]{2,1,0:T(8,128)S(1)}, f32[32,20,128]{2,1,0:T(8,128)S(1)}, u32[]{:S(2)}, u32[]{:S(2)}) collective-permute-start(f32[32,20,128]{2,1,0:T(8,128)S(1)} %get-tuple-element.9), channel_id=1, source_target_pairs={{0,1},{1,2},{2,3},{3,4},{4,5},{5,6},{6,7},{8,9},{9,10},{10,11},{11... | collective-permute-start | bytes 983048 | tf_op jit(solution)/shard_map/ppermute | solution.py:331
  4.4 21.7 %collective-permute-start.1 = (f32[32,20,128]{2,1,0:T(8,128)S(1)}, f32[32,20,128]{2,1,0:T(8,128)S(1)}, u32[]{:S(2)}, u32[]{:S(2)}) collective-permute-start(f32[32,20,128]{2,1,0:T(8,128)S(1)} %get-tuple-element.10), channel_id=1, source_target_pairs={{1,0},{2,1},{3,2},{4,3},{5,4},{6,5},{7,6},{9,8},{10,9},{11,10},{12... | collective-permute-start | bytes 983048 | tf_op jit(solution)/shard_map/ppermute | solution.py:332
  18.8 7.3 %copy-start = (f32[1,32,32,128]{3,2,1,0:T(8,128)S(1)}, f32[1,32,32,128]{3,2,1,0:T(8,128)}, u32[]{:S(2)}) copy-start(f32[1,32,32,128]{3,2,1,0:T(8,128)} %param.10) | copy-start | bytes 1572868
  53.0 13.6 %copy-start.2 = (f32[8,32,128]{2,1,0:T(8,128)S(1)}, f32[8,32,128]{2,1,0:T(8,128)}, u32[]{:S(2)}) copy-start(f32[8,32,128]{2,1,0:T(8,128)} %get-tuple-element.8) | copy-start | bytes 393220
where the time goes:
time: 68.1 us; the launch traced here: 67.4 us
  Pallas kernels  32.9 us (48%)
  blocking collectives  12.6 us (19%)
  other arithmetic  10 us (15%)
  starting transfers between devices  6.18 us (9%)
  local copies, waits for them, and re-layouts  3.56 us (5%)
  between operations  2.09 us (3%)
    pallas_call x1, Pallas kernels, shards(): pl.pallas_call(functools.partial(main_kernel, dims, places, voxels), out_...  25.6 us
    all_to_all x1, blocking collectives, shards(): lax.all_to_all(scores, 'rot', split_axis=0, concat_axis=0, tiled=True)  12.6 us
    pallas_call x1, Pallas kernels, shards(): pl.pallas_call(functools.partial(template_kernel, length_y), out_shape=ja...  7.29 us
    ppermute x1, starting transfers between devices, halo(): lax.ppermute(lax.slice_in_dim(block, size - HALF, size, axis=axis), 'tile...  3.12 us
    ppermute x1, starting transfers between devices, halo(): lax.ppermute(lax.slice_in_dim(block, 0, HALF, axis=axis), 'tile', down)  3.06 us
    reduce_sum x1, other arithmetic, normalize(): spread = jnp.sqrt(jnp.sum(centred * centred) / voxel_count + EPSILON)  2.36 us
    reduce_sum x1, other arithmetic, normalize(): centre = jnp.sum(template * sphere_mask) / voxel_count  2.35 us
    div x1, other arithmetic, normalize(): return centred / spread  2.22 us
  transfers between devices with their start and end apart: 2, of which 0 were waited for; matrix products, arithmetic and copies ran while one was open for 14% of the time, Pallas kernels for 11%

commit v1 on v0

--- a/solution.py
+++ b/solution.py
@@ -52,9 +52,11 @@
     return 2.0 * math.pi * ((np.asarray(rows)[:, None] * np.asarray(columns)[None, :]) % length) / length
 
 
-def y_forward(length, inputs):
-    theta = angles(length, np.arange(length), np.arange(length))[:, : min(inputs, length)]
-    return left_table(np.concatenate([wide(np.cos(theta), 1, inputs), wide(np.sin(theta), 1, inputs)], axis=0))
+def y_forward(length, inputs, offset):
+    y = np.arange(inputs) - offset
+    theta = angles(length, np.arange(length), y)
+    inside = ((y >= 0) & (y < length))[None, :]
+    return left_table(np.concatenate([np.cos(theta) * inside, np.sin(theta) * inside], axis=0))
 
 
 def z_forward(length, inputs, freqs):
@@ -158,12 +160,14 @@
     return jnp.dot(a, b, preferred_element_type=jnp.float32)
 
 
-def planes(pair, ly, tz, length_y):
-    o = dot(ly, pieces(pair, 0))
-    g = jnp.concatenate([o[:, :LANES], o[:, LANES:]], axis=0)
-    h = dot(pieces(g, 1), tz)
+def planes(pairs, ly, tz, length_y):
+    flat = []
+    for pair in pairs:
+        o = dot(ly, pieces(pair, 0))
+        flat += [o[:, :LANES], o[:, LANES:]]
+    h = dot(pieces(jnp.concatenate(flat, axis=0), 1), tz)
     outs = []
-    for which in range(2):
+    for which in range(2 * len(pairs)):
         base = 2 * length_y * which
         c = h[base : base + length_y]
         s = h[base + length_y : base + 2 * length_y]
@@ -171,16 +175,139 @@
     return outs
 
 
-def template_kernel(length_y, grid_ref, ly_ref, tz_ref, out_ref):
-    def step(pair, carry):
-        both = jnp.concatenate([grid_ref[2 * pair], grid_ref[2 * pair + 1]], axis=1)
-        outs = planes(both, ly_ref[...], tz_ref[...], length_y)
-        for which, (re, im) in enumerate(outs):
-            out_ref[2 * pair + which, :, :LANES] = re
-            out_ref[2 * pair + which, :, LANES:] = im
+def template_kernel(
+    length_y, across, rim, voxels, grid_ref, block_ref, ly_ref, tz_ref, out_ref, ext_ref, send_sem, recv_sem
+):
+    tile = lax.axis_index("tile")
+    column = lax.rem(tile, across)
+    before, after = column > 0, column < across - 1
+    size_y = block_ref.shape[1]
+    barrier = pltpu.get_barrier_semaphore()
+
+    def to_next():
+        return pltpu.make_async_remote_copy(
+            src_ref=block_ref.at[:, pl.ds(size_y - rim, rim), :],
+            dst_ref=ext_ref.at[:, pl.ds(0, rim), :],
+            send_sem=send_sem.at[0],
+            recv_sem=recv_sem.at[0],
+            device_id={"tile": tile + 1},
+            device_id_type=pl.DeviceIdType.MESH,
+        )
+
+    def to_previous():
+        return pltpu.make_async_remote_copy(
+            src_ref=block_ref.at[:, pl.ds(0, rim), :],
+            dst_ref=ext_ref.at[:, pl.ds(rim + size_y, rim), :],
+            send_sem=send_sem.at[1],
+            recv_sem=recv_sem.at[1],
+            device_id={"tile": tile - 1},
+            device_id_type=pl.DeviceIdType.MESH,
+        )
+
+    @pl.when(before)
+    def _():
+        pl.semaphore_signal(barrier, inc=1, device_id={"tile": tile - 1}, device_id_type=pl.DeviceIdType.MESH)
+
+    @pl.when(after)
+    def _():
+        pl.semaphore_signal(barrier, inc=1, device_id={"tile": tile + 1}, device_id_type=pl.DeviceIdType.MESH)
+
+    shape = grid_ref.shape[1:]
+    odd_y = 2 * lax.broadcasted_iota(jnp.int32, shape, 0) - (TMPL - 1)
+    odd_z = 2 * lax.broadcasted_iota(jnp.int32, shape, 1) - (TMPL - 1)
+    plane_sq = odd_y * odd_y + odd_z * odd_z
+
+    def masked(q, centre):
+        odd_x = 2 * q - (TMPL - 1)
+        inside = plane_sq + odd_x * odd_x <= TMPL * TMPL
+        return jnp.where(inside, grid_ref[q].astype(jnp.float32) - centre, 0.0)
+
+    zeros = jnp.zeros(shape, jnp.float32)
+    total = lax.fori_loop(0, TMPL, lambda q, held: held + masked(q, 0.0), zeros, unroll=4)
+    centre = jnp.sum(total) / voxels
+
+    def add_square(q, held):
+        value = masked(q, centre)
+        return held + value * value
+
+    squares = jnp.sum(lax.fori_loop(0, TMPL, add_square, zeros, unroll=4), keepdims=True)
+    scale = 1.0 / jnp.sqrt(squares / voxels + EPSILON)
+
+    pl.semaphore_wait(barrier, before.astype(jnp.int32) + after.astype(jnp.int32))
+
+    @pl.when(before)
+    def _():
+        to_previous().start()
+
+    @pl.when(after)
+    def _():
+        to_next().start()
+
+    ext_ref[:, rim : rim + size_y, :] = block_ref[...]
+    nothing = jnp.zeros((block_ref.shape[0], rim, LANES), jnp.float32)
+
+    @pl.when(jnp.logical_not(before))
+    def _():
+        ext_ref[:, :rim, :] = nothing
+
+    @pl.when(jnp.logical_not(after))
+    def _():
+        ext_ref[:, rim + size_y :, :] = nothing
+
+    group = 4
+
+    def step(index, carry):
+        pairs = []
+        for i in range(group):
+            q = 2 * (index * group + i)
+            pairs.append(jnp.concatenate([masked(q, centre) * scale, masked(q + 1, centre) * scale], axis=1))
+        for which, (re, im) in enumerate(planes(pairs, ly_ref[...], tz_ref[...], length_y)):
+            out_ref[2 * group * index + which, :, :LANES] = re
+            out_ref[2 * group * index + which, :, LANES:] = im
         return carry
 
-    lax.fori_loop(0, TMPL // 2, step, 0, unroll=2)
+    lax.fori_loop(0, TMPL // (2 * group), step, 0)
+
+    @pl.when(before)
+    def _():
+        to_previous().wait_send()
+        to_next().wait_recv()
+
+    @pl.when(after)
+    def _():
+        to_next().wait_send()
+        to_previous().wait_recv()
+
+
+def exchange_kernel(rots, score_ref, scale_ref, out_ref, others, send_sem, recv_sem):
+    me = lax.axis_index("rot")
+    rows = scale_ref.shape[0]
+    barrier = pltpu.get_barrier_semaphore()
+    peers = [lax.rem(me + d, rots) for d in range(1, rots)]
+    for peer in peers:
+        pl.semaphore_signal(barrier, inc=1, device_id={"rot": peer}, device_id_type=pl.DeviceIdType.MESH)
+    pl.semaphore_wait(barrier, rots - 1)
+    copies = []
+    for d, peer in enumerate(peers):
+        copy = pltpu.make_async_remote_copy(
+            src_ref=score_ref.at[pl.ds(peer * rows, rows)],
+            dst_ref=others.at[d],
+            send_sem=send_sem.at[d],
+            recv_sem=recv_sem.at[d],
+            device_id={"rot": peer},
+            device_id_type=pl.DeviceIdType.MESH,
+        )
+        copy.start()
+        copies.append(copy)
+    scale = scale_ref[...]
+    scores = [score_ref[pl.ds(me * rows, rows)] * scale]
+    for copy in copies:
+        copy.wait()
+    for d in range(rots - 1):
+        scores.append(others[d] * scale)
+    largest = functools.reduce(jnp.maximum, scores)
+    total = functools.reduce(jnp.add, [jnp.exp(score - largest) for score in scores])
+    out_ref[...] = largest + jnp.log(total)
 
 
 def main_kernel(
@@ -194,15 +321,17 @@
     fetch = pltpu.make_async_copy(mhat_hbm, mhat, sem)
     fetch.start()
 
-    def forward(x, carry):
-        v = ext_ref[x]
-        outs = planes(jnp.concatenate([v, v * v], axis=1), ly_ref[...], tz_ref[...], length_y)
-        for which, (re, im) in enumerate(outs):
-            fields[which, x, :, :LANES] = re
-            fields[which, x, :, LANES:] = im
+    def forward(step, carry):
+        pairs = []
+        for i in range(4):
+            v = ext_ref[4 * step + i]
+            pairs.append(jnp.concatenate([v, v * v], axis=1))
+        for which, (re, im) in enumerate(planes(pairs, ly_ref[...], tz_ref[...], length_y)):
+            fields[which % 2, 4 * step + which // 2, :, :LANES] = re
+            fields[which % 2, 4 * step + which // 2, :, LANES:] = im
         return carry
 
-    lax.fori_loop(0, size_in, forward, 0, unroll=2)
+    lax.fori_loop(0, size_in // 4, forward, 0)
     rows[:, length_y:, :] = jnp.zeros((rows.shape[0], padded - length_y, 2 * LANES), jnp.float32)
     fetch.wait()
 
@@ -291,7 +420,7 @@
 
     lax.fori_loop(0, length_y // 8, block, 0)
 
-    group = 4
+    group = 8
 
     def inverse(step, carry):
         flat = []
@@ -314,23 +443,13 @@
     scale_ref[...] = SHARPNESS / (math.sqrt(voxels) * std)
 
 
-def normalize(flat_grid, sphere_mask, voxel_count):
-    template = flat_grid.astype(jnp.float32).reshape(TMPL, TMPL, TMPL)
-    centre = jnp.sum(template * sphere_mask) / voxel_count
-    centred = (template - centre) * sphere_mask
-    spread = jnp.sqrt(jnp.sum(centred * centred) / voxel_count + EPSILON)
-    return centred / spread
-
-
-def halo(block, distance, across, axis):
+def row_halo(block, across):
     tiles = lax.axis_size("tile")
-    stays = lambda t: distance > 1 or t % across != 0
-    up = [(t - distance, t) for t in range(distance, tiles) if distance >= across or t % across != 0]
+    up = [(t - across, t) for t in range(across, tiles)]
     down = [(t, s) for s, t in up]
-    size = block.shape[axis]
-    lower = lax.ppermute(lax.slice_in_dim(block, size - HALF, size, axis=axis), "tile", up)
-    upper = lax.ppermute(lax.slice_in_dim(block, 0, HALF, axis=axis), "tile", down)
-    return lower, upper
+    lower = lax.ppermute(block[block.shape[0] - HALF :], "tile", up)
+    upper = lax.ppermute(block[:HALF], "tile", down)
+    return jnp.concatenate([lower, block, upper], axis=0)
 
 
 def shards(volume, templates, rot_ids):
@@ -342,8 +461,7 @@
     size_x, size_y, size_z = block.shape
     inner = size_x // rots
     if down > 1:
-        lower, upper = halo(block, across, across, 0)
-        block = jnp.concatenate([lower, block, upper], axis=0)
+        block = row_halo(block, across)
         length_x = size_x + TMPL
         places = tuple(range(TMPL))
     else:
@@ -358,27 +476,25 @@
 
     mask = sphere()
     voxels = float(mask.sum())
-    if across > 1:
-        lower, upper = halo(block, 1, across, 1)
-    else:
-        lower = upper = jnp.zeros((size_in, HALF, size_z), jnp.float32)
-    bottom = jnp.zeros((size_in, padded - length_y, size_z), jnp.float32)
-    extended = jnp.concatenate([lower, block, upper, bottom], axis=1)
-
+    rim = -(-HALF // 8) * 8
+    reach = size_y + 2 * rim
     tz = jnp.asarray(z_forward(length_z, LANES, freqs))
-    kernel = normalize(templates[rot_ids[0]], jnp.asarray(mask, jnp.float32), voxels)
     kernel_rows = 48
-    kernel = jnp.pad(kernel, ((0, 0), (0, kernel_rows - TMPL), (0, LANES - TMPL)))
+    grid = templates[rot_ids[0]].reshape(TMPL, TMPL, TMPL)
+    grid = jnp.pad(grid, ((0, 0), (0, kernel_rows - TMPL), (0, LANES - TMPL)))
     vmem = pl.BlockSpec(memory_space=pltpu.VMEM)
-    khat = pl.pallas_call(
-        functools.partial(template_kernel, length_y),
-        out_shape=jax.ShapeDtypeStruct((TMPL, length_y, 2 * LANES), jnp.float32),
-        in_specs=[vmem] * 3,
-        out_specs=vmem,
-        compiler_params=pltpu.CompilerParams(vmem_limit_bytes=VMEM),
-        cost_estimate=pl.CostEstimate(flops=4 * 10**9, bytes_accessed=4 * 10**6, transcendentals=0),
+    khat, extended = pl.pallas_call(
+        functools.partial(template_kernel, length_y, across, rim, voxels),
+        out_shape=(
+            jax.ShapeDtypeStruct((TMPL, length_y, 2 * LANES), jnp.float32),
+            jax.ShapeDtypeStruct((size_in, reach, size_z), jnp.float32),
+        ),
+        in_specs=[vmem] * 4,
+        out_specs=(vmem, vmem),
+        scratch_shapes=[pltpu.SemaphoreType.DMA((2,)), pltpu.SemaphoreType.DMA((2,))],
+        compiler_params=pltpu.CompilerParams(vmem_limit_bytes=VMEM, collective_id=0, has_side_effects=True),
         name="template_spectrum",
-    )(kernel, jnp.asarray(y_forward(length_y, kernel_rows)), tz)
+    )(grid, block, jnp.asarray(y_forward(length_y, kernel_rows, 0)), tz)
 
     mhat = jnp.asarray(mask_spectrum(places, length_x, length_y, length_z, freqs))
     angle = (jnp.arange(outer) * lax.axis_index("rot") % outer).astype(jnp.float32) * (2.0 * math.pi / outer)
@@ -408,14 +524,24 @@
         name="correlate",
     )(
         extended, khat, mhat, phase,
-        jnp.asarray(y_forward(length_y, padded)), tz,
+        jnp.asarray(y_forward(length_y, reach, rim - HALF)), tz,
         jnp.asarray(y_inverse(length_y, padded, size_y)),
         jnp.asarray(z_inverse(length_z, size_z, freqs, length_x)),
     )
-    gathered = lax.all_to_all(scores, "rot", split_axis=0, concat_axis=0, tiled=True)
-    gathered = gathered.reshape(rots, inner, size_y, size_z) * scale[None]
-    largest = jnp.max(gathered, axis=0)
-    return (largest + jnp.log(jnp.sum(jnp.exp(gathered - largest[None]), axis=0)))[None]
+    result = pl.pallas_call(
+        functools.partial(exchange_kernel, rots),
+        out_shape=jax.ShapeDtypeStruct((inner, size_y, size_z), jnp.float32),
+        in_specs=[vmem, vmem],
+        out_specs=vmem,
+        scratch_shapes=[
+            pltpu.VMEM((rots - 1, inner, size_y, size_z), jnp.float32),
+            pltpu.SemaphoreType.DMA((rots - 1,)),
+            pltpu.SemaphoreType.DMA((rots - 1,)),
+        ],
+        compiler_params=pltpu.CompilerParams(vmem_limit_bytes=VMEM, collective_id=1, has_side_effects=True),
+        name="exchange",
+    )(scores, scale)
+    return result[None]
 
 
 def solution(mesh):

time: 68.1 us -> 62.4 us (0.916)
  Pallas kernels: 32.9 us -> 55.7 us
  blocking collectives: 12.6 us -> 0 us
  other arithmetic: 10 us -> 0.06 us
  starting transfers between devices: 6.18 us -> 0 us
  local copies, waits for them, and re-layouts: 3.56 us -> 5.74 us
  between operations: 2.09 us -> 0.7 us
    pallas_call x1 -> x2, Pallas kernels: 7.29 us -> 33.9 us  [the longest x1 23.6 us: shards(): pl.pallas_call(functools.partial(template_kernel, length_y, across, rim,...]
    all_to_all x1 -> x0, blocking collectives: 12.6 us -> none  [shards(): lax.all_to_all(scores, 'rot', split_axis=0, concat_axis=0, tiled=True)]
    ppermute x2 -> x0, starting transfers between devices: 6.18 us -> none  [the longest x1 3.12 us: halo(): lax.ppermute(lax.slice_in_dim(block, size - HALF, size, axis=axis), 'tile...]
    reduce_sum x3 -> x0, other arithmetic: 4.81 us -> none  [the longest x1 2.36 us: normalize(): spread = jnp.sqrt(jnp.sum(centred * centred) / voxel_count + EPSILON)]
    pallas_call x1, Pallas kernels: 25.6 us -> 21.7 us  [shards(): pl.pallas_call(functools.partial(main_kernel, dims, places, voxels), out_...]
    div x1 -> x0, other arithmetic: 2.22 us -> none  [normalize(): return centred / spread]
    dynamic_slice x0 -> x1, local copies, waits for them, and re-layouts: none -> 2.01 us  [shards(): grid = templates[rot_ids[0]].reshape(TMPL, TMPL, TMPL)]
    unnamed x6 -> x1, local copies, waits for them, and re-layouts: 0.01 us -> 1.57 us
  transfers between devices with their start and end apart: 2 -> 0, of which waited for: 0 -> 0; matrix products, arithmetic and copies ran while one was open for 14% -> 0% of each run, Pallas kernels for 11% -> 0%
where the time goes in v1:
time: 62.4 us; the launch traced here: 62.2 us
  Pallas kernels  55.7 us (89%)
  local copies, waits for them, and re-layouts  5.74 us (9%)
  between operations  0.7 us (1%)
    pallas_call x1, Pallas kernels, shards(): pl.pallas_call(functools.partial(template_kernel, length_y, across, rim,...  23.6 us
    pallas_call x1, Pallas kernels, shards(): pl.pallas_call(functools.partial(main_kernel, dims, places, voxels), out_...  21.7 us
    pallas_call x1, Pallas kernels, shards(): pl.pallas_call(functools.partial(exchange_kernel, rots), out_shape=jax.Sh...  10.3 us
    dynamic_slice x1, local copies, waits for them, and re-layouts, shards(): grid = templates[rot_ids[0]].reshape(TMPL, TMPL, TMPL)  2.01 us
    unnamed x1, local copies, waits for them, and re-layouts  1.57 us

profile of v1, /device:TPU:9, one launch (start us, length us, event | category | flops | bytes accessed | tf_op | source)
XLA Modules:
  0.0 62.2 jit_solution(6943247716365210728)
XLA Ops:
  0.7 0.1 fusion.3
  0.7 0.7 %copy.10.phase_ref = f32[8,2]{1,0:T(8,128)} copy(f32[8,2]{0,1:T(2,128)S(1)} %pad_maximum_fusion) | data formatting | bytes 128 | tf_op jit(solution)/shard_map/stack | solution.py:501
  1.4 2.0 %dynamic-slice_reduce_fusion = bf16[64000]{0:T(1024)(128)(2,1)S(1)} fusion(bf16[32,64000]{1,0:T(8,128)(2,1)} %param.10, s32[]{:T(128)S(6)} %select_n.21), kind=kLoop, calls=%fused_computation | loop fusion | bytes 256004 | tf_op jit(solution)/shard_map/dynamic_slice | solution.py:483
  3.4 0.6 reshape_squeeze.3
  4.0 0.9 %pad.4.grid_ref = bf16[40,48,128]{2,1,0:T(8,128)(2,1)} pad(bf16[40,40,40]{2,1,0:T(8,128)(2,1)S(1)} %reshape_squeeze.3, bf16[]{:T(256)} %constant.34.clone.1), padding=0_0x0_8x0_88 | pad | bytes 619522 | tf_op jit(solution)/shard_map/jit(_pad)/pad | solution.py:484
  4.9 23.6 %template_spectrum.1 = (f32[40,72,256]{2,1,0:T(8,128)}, f32[32,80,128]{2,1,0:T(8,128)}) custom-call(bf16[40,48,128]{2,1,0:T(8,128)(2,1)} %pad.4.grid_ref, f32[32,32,128]{2,1,0:T(8,128)} %bitcast.6, bf16[144,144]{1,0:T(8,128)(2,1)} %constant.40.clone.ly_ref, bf16[384,256]{1,0:T(8,128)(2,1)} %constant.39.clone.tz_ref), custom_call_target="tpu_custom_call" | custom-call | tf_op jit(solution)/shard_map/template_spectrum/pallas_call | solution.py:486
  28.5 21.7 %correlate.1 = (f32[32,32,128]{2,1,0:T(8,128)}, f32[8,32,128]{2,1,0:T(8,128)}) custom-call(f32[32,80,128]{2,1,0:T(8,128)} %get-tuple-element.9.ext_ref, f32[40,72,256]{2,1,0:T(8,128)} %get-tuple-element.10.khat_ref, f32[64,72,256]{2,1,0:T(8,128)} %constant.41.clone.mhat_hbm, f32[8,2]{1,0:T(8,128)} %copy.10.phase_ref, ...), custom_call_target="tpu_custom_call" | custom-call | tf_op jit(solution)/shard_map/correlate/pallas_call | solution.py:503
  50.3 10.3 %exchange.1 = f32[8,32,128]{2,1,0:T(8,128)} custom-call(f32[32,32,128]{2,1,0:T(8,128)} %get-tuple-element.11.score_ref, f32[8,32,128]{2,1,0:T(8,128)} %get-tuple-element.12.scale_ref), custom_call_target="tpu_custom_call" | custom-call | tf_op jit(solution)/shard_map/exchange/pallas_call | solution.py:531
  60.6 1.6 %copy.13 = f32[1,8,32,128]{3,2,1,0:T(8,128)} copy(f32[1,8,32,128]{3,2,1,0:T(8,128)} %bitcast.7) | data formatting | bytes 262144
  (1 shorter events, 0.0 us)

commit v2 on v1

--- a/solution.py
+++ b/solution.py
@@ -176,9 +176,14 @@
 
 
 def template_kernel(
-    length_y, across, rim, voxels, grid_ref, block_ref, ly_ref, tz_ref, out_ref, ext_ref, send_sem, recv_sem
+    length_y, across, rim, voxels, raw_ref, block_ref, ly_ref, tz_ref, out_ref, ext_ref,
+    grid_ref, send_sem, recv_sem,
 ):
     tile = lax.axis_index("tile")
+    core = lax.rem(lax.axis_index("rot"), 2)
+    mate = lax.axis_index("rot") + 1 - 2 * core
+    depth = block_ref.shape[0] // 2
+    half = pl.ds(core * depth, depth)
     column = lax.rem(tile, across)
     before, after = column > 0, column < across - 1
     size_y = block_ref.shape[1]
@@ -186,8 +191,8 @@
 
     def to_next():
         return pltpu.make_async_remote_copy(
-            src_ref=block_ref.at[:, pl.ds(size_y - rim, rim), :],
-            dst_ref=ext_ref.at[:, pl.ds(0, rim), :],
+            src_ref=block_ref.at[half, pl.ds(size_y - rim, rim), :],
+            dst_ref=ext_ref.at[half, pl.ds(0, rim), :],
             send_sem=send_sem.at[0],
             recv_sem=recv_sem.at[0],
             device_id={"tile": tile + 1},
@@ -196,14 +201,26 @@
 
     def to_previous():
         return pltpu.make_async_remote_copy(
-            src_ref=block_ref.at[:, pl.ds(0, rim), :],
-            dst_ref=ext_ref.at[:, pl.ds(rim + size_y, rim), :],
+            src_ref=block_ref.at[half, pl.ds(0, rim), :],
+            dst_ref=ext_ref.at[half, pl.ds(rim + size_y, rim), :],
             send_sem=send_sem.at[1],
             recv_sem=recv_sem.at[1],
             device_id={"tile": tile - 1},
             device_id_type=pl.DeviceIdType.MESH,
         )
 
+    def to_mate(start, slot):
+        return pltpu.make_async_remote_copy(
+            src_ref=ext_ref.at[half, pl.ds(start, rim), :],
+            dst_ref=ext_ref.at[half, pl.ds(start, rim), :],
+            send_sem=send_sem.at[slot],
+            recv_sem=recv_sem.at[slot],
+            device_id={"rot": mate},
+            device_id_type=pl.DeviceIdType.MESH,
+        )
+
+    pl.semaphore_signal(barrier, inc=1, device_id={"rot": mate}, device_id_type=pl.DeviceIdType.MESH)
+
     @pl.when(before)
     def _():
         pl.semaphore_signal(barrier, inc=1, device_id={"tile": tile - 1}, device_id_type=pl.DeviceIdType.MESH)
@@ -212,6 +229,8 @@
     def _():
         pl.semaphore_signal(barrier, inc=1, device_id={"tile": tile + 1}, device_id_type=pl.DeviceIdType.MESH)
 
+    grid_ref[...] = jnp.zeros(grid_ref.shape, jnp.float32)
+    grid_ref[:, :TMPL, :TMPL] = raw_ref[...].astype(jnp.float32)
     shape = grid_ref.shape[1:]
     odd_y = 2 * lax.broadcasted_iota(jnp.int32, shape, 0) - (TMPL - 1)
     odd_z = 2 * lax.broadcasted_iota(jnp.int32, shape, 1) - (TMPL - 1)
@@ -220,7 +239,7 @@
     def masked(q, centre):
         odd_x = 2 * q - (TMPL - 1)
         inside = plane_sq + odd_x * odd_x <= TMPL * TMPL
-        return jnp.where(inside, grid_ref[q].astype(jnp.float32) - centre, 0.0)
+        return jnp.where(inside, grid_ref[q] - centre, 0.0)
 
     zeros = jnp.zeros(shape, jnp.float32)
     total = lax.fori_loop(0, TMPL, lambda q, held: held + masked(q, 0.0), zeros, unroll=4)
@@ -233,7 +252,7 @@
     squares = jnp.sum(lax.fori_loop(0, TMPL, add_square, zeros, unroll=4), keepdims=True)
     scale = 1.0 / jnp.sqrt(squares / voxels + EPSILON)
 
-    pl.semaphore_wait(barrier, before.astype(jnp.int32) + after.astype(jnp.int32))
+    pl.semaphore_wait(barrier, before.astype(jnp.int32) + after.astype(jnp.int32) + 1)
 
     @pl.when(before)
     def _():
@@ -272,11 +291,21 @@
     def _():
         to_previous().wait_send()
         to_next().wait_recv()
+        to_mate(0, 2).start()
 
     @pl.when(after)
     def _():
         to_next().wait_send()
         to_previous().wait_recv()
+        to_mate(rim + size_y, 3).start()
+
+    @pl.when(before)
+    def _():
+        to_mate(0, 2).wait()
+
+    @pl.when(after)
+    def _():
+        to_mate(rim + size_y, 3).wait()
 
 
 def exchange_kernel(rots, score_ref, scale_ref, out_ref, others, send_sem, recv_sem):
@@ -312,14 +341,19 @@
 
 def main_kernel(
     dims, places, voxels,
-    ext_ref, khat_ref, mhat_hbm, phase_ref, ly_ref, tz_ref, iy_ref, iz_ref,
+    ext_ref, khat_hbm, mhat_hbm, phase_ref, ly_ref, tz_ref, iy_ref, iz_ref,
     score_ref, scale_ref,
-    fields, mhat, stage, mixed, rows, local, sem,
+    fields, khat_ref, mhat, stage, mixed, rows, local, sem,
 ):
     size_in, length_y, padded, size_x, size_y, inner, outer = dims
     length_x = inner * outer
-    fetch = pltpu.make_async_copy(mhat_hbm, mhat, sem)
-    fetch.start()
+    fetches = [
+        pltpu.make_async_copy(khat_hbm, khat_ref, sem.at[0]),
+        pltpu.make_async_copy(mhat_hbm, mhat, sem.at[1]),
+    ]
+    for fetch in fetches:
+        fetch.start()
+    me = lax.axis_index("rot")
 
     def forward(step, carry):
         pairs = []
@@ -333,7 +367,8 @@
 
     lax.fori_loop(0, size_in // 4, forward, 0)
     rows[:, length_y:, :] = jnp.zeros((rows.shape[0], padded - length_y, 2 * LANES), jnp.float32)
-    fetch.wait()
+    for fetch in fetches:
+        fetch.wait()
 
     def block(r, carry):
         at = pl.ds(pl.multiple_of(r * 8, 8), 8)
@@ -407,7 +442,7 @@
             for slot in (1, 2):
                 re_sum = None
                 for k1, (re, im) in enumerate(load(slot)):
-                    c, s = phase_ref[k1, 0], phase_ref[k1, 1]
+                    c, s = phase_ref[me, 2 * k1], phase_ref[me, 2 * k1 + 1]
                     re_part, im_part = re * c - im * s, re * s + im * c
                     if re_sum is None:
                         re_sum, im_sum = re_part, im_part
@@ -481,7 +516,6 @@
     tz = jnp.asarray(z_forward(length_z, LANES, freqs))
     kernel_rows = 48
     grid = templates[rot_ids[0]].reshape(TMPL, TMPL, TMPL)
-    grid = jnp.pad(grid, ((0, 0), (0, kernel_rows - TMPL), (0, LANES - TMPL)))
     vmem = pl.BlockSpec(memory_space=pltpu.VMEM)
     khat, extended = pl.pallas_call(
         functools.partial(template_kernel, length_y, across, rim, voxels),
@@ -491,14 +525,18 @@
         ),
         in_specs=[vmem] * 4,
         out_specs=(vmem, vmem),
-        scratch_shapes=[pltpu.SemaphoreType.DMA((2,)), pltpu.SemaphoreType.DMA((2,))],
+        scratch_shapes=[
+            pltpu.VMEM((TMPL, kernel_rows, LANES), jnp.float32),
+            pltpu.SemaphoreType.DMA((4,)),
+            pltpu.SemaphoreType.DMA((4,)),
+        ],
         compiler_params=pltpu.CompilerParams(vmem_limit_bytes=VMEM, collective_id=0, has_side_effects=True),
         name="template_spectrum",
     )(grid, block, jnp.asarray(y_forward(length_y, kernel_rows, 0)), tz)
 
     mhat = jnp.asarray(mask_spectrum(places, length_x, length_y, length_z, freqs))
-    angle = (jnp.arange(outer) * lax.axis_index("rot") % outer).astype(jnp.float32) * (2.0 * math.pi / outer)
-    phase = jnp.stack([jnp.cos(angle), jnp.sin(angle)], axis=1)
+    turns = angles(outer, np.arange(rots), np.arange(outer))
+    phase = jnp.asarray(np.stack([np.cos(turns), np.sin(turns)], axis=2).reshape(rots, 2 * outer).astype(np.float32))
     dims = (size_in, length_y, padded, size_x, size_y, inner, outer)
     scores, scale = pl.pallas_call(
         functools.partial(main_kernel, dims, places, voxels),
@@ -507,18 +545,19 @@
             jax.ShapeDtypeStruct((inner, size_y, size_z), jnp.float32),
         ),
         in_specs=[
-            vmem, vmem, pl.BlockSpec(memory_space=pl.ANY), pl.BlockSpec(memory_space=pltpu.SMEM),
+            vmem, pl.BlockSpec(memory_space=pl.ANY), pl.BlockSpec(memory_space=pl.ANY), pl.BlockSpec(memory_space=pltpu.SMEM),
             vmem, vmem, vmem, vmem,
         ],
         out_specs=(vmem, vmem),
         scratch_shapes=[
             pltpu.VMEM((2, size_in, length_y, 2 * LANES), jnp.float32),
+            pltpu.VMEM((TMPL, length_y, 2 * LANES), jnp.float32),
             pltpu.VMEM((length_x, length_y, 2 * LANES), jnp.float32),
             pltpu.VMEM((3, length_x, 8, 2 * LANES), jnp.float32),
             pltpu.VMEM((3, length_x, 8, 2 * LANES), jnp.float32),
             pltpu.VMEM((size_x + 2 * inner, padded, 2 * LANES), jnp.float32),
             pltpu.VMEM((size_x + 2 * inner, size_y, size_z), jnp.float32),
-            pltpu.SemaphoreType.DMA,
+            pltpu.SemaphoreType.DMA((2,)),
         ],
         compiler_params=pltpu.CompilerParams(vmem_limit_bytes=VMEM),
         name="correlate",

time: 62.4 us -> 53.5 us (0.86)
  Pallas kernels: 55.7 us -> 47.6 us
  local copies, waits for them, and re-layouts: 5.74 us -> 4.94 us
    pallas_call x1, Pallas kernels: 23.6 us -> 16.6 us  [shards(): pl.pallas_call(functools.partial(template_kernel, length_y, across, rim,...]
    pad x1 -> x0, local copies, waits for them, and re-layouts: 0.88 us -> none  [shards(): grid = jnp.pad(grid, ((0, 0), (0, kernel_rows - TMPL), (0, LANES - TMPL)))]
    another operation x1, local copies, waits for them, and re-layouts: 0.61 us -> 1.36 us  [shards(): grid = templates[rot_ids[0]].reshape(TMPL, TMPL, TMPL)]
    pallas_call x1, Pallas kernels: 21.7 us -> 21 us  [shards(): pl.pallas_call(functools.partial(main_kernel, dims, places, voxels), out_...]
    another operation x1 -> x0, local copies, waits for them, and re-layouts: 0.68 us -> none  [shards(): phase = jnp.stack([jnp.cos(angle), jnp.sin(angle)], axis=1)]
where the time goes in v2:
time: 53.5 us; the launch traced here: 53.2 us
  Pallas kernels  47.6 us (89%)
  local copies, waits for them, and re-layouts  4.94 us (9%)
  between operations  0.68 us (1%)
    pallas_call x1, Pallas kernels, shards(): pl.pallas_call(functools.partial(main_kernel, dims, places, voxels), out_...  21 us
    pallas_call x1, Pallas kernels, shards(): pl.pallas_call(functools.partial(template_kernel, length_y, across, rim,...  16.6 us
    pallas_call x1, Pallas kernels, shards(): pl.pallas_call(functools.partial(exchange_kernel, rots), out_shape=jax.Sh...  9.99 us
    dynamic_slice x1, local copies, waits for them, and re-layouts, shards(): grid = templates[rot_ids[0]].reshape(TMPL, TMPL, TMPL)  2.01 us
    unnamed x1, local copies, waits for them, and re-layouts  1.57 us
    another operation x1, local copies, waits for them, and re-layouts, shards(): grid = templates[rot_ids[0]].reshape(TMPL, TMPL, TMPL)  1.36 us

profile of v2, /device:TPU:9, one launch (start us, length us, event | category | flops | bytes accessed | tf_op | source)
XLA Modules:
  0.0 53.2 jit_solution(2075238254802561212)
XLA Ops:
  0.7 2.0 %dynamic-slice_reduce_fusion = bf16[64000]{0:T(1024)(128)(2,1)S(1)} fusion(bf16[32,64000]{1,0:T(8,128)(2,1)} %param.11, s32[]{:T(128)S(6)} %select_n.3), kind=kLoop, calls=%fused_computation | loop fusion | bytes 256004 | tf_op jit(solution)/shard_map/dynamic_slice | solution.py:518
  2.7 1.4 %reshape_squeeze.3.raw_ref = bf16[40,40,40]{2,1,0:T(8,128)(2,1)} reshape(bf16[64000]{0:T(1024)(128)(2,1)S(1)} %dynamic-slice_reduce_fusion) | data formatting | bytes 256000 | tf_op jit(solution)/shard_map/reshape;squeeze | solution.py:518
  4.0 16.6 %template_spectrum.1 = (f32[40,72,256]{2,1,0:T(8,128)}, f32[32,80,128]{2,1,0:T(8,128)}) custom-call(bf16[40,40,40]{2,1,0:T(8,128)(2,1)} %reshape_squeeze.3.raw_ref, f32[32,32,128]{2,1,0:T(8,128)} %bitcast.6, bf16[144,144]{1,0:T(8,128)(2,1)} %constant.19.clone.ly_ref, bf16[384,256]{1,0:T(8,128)(2,1)} %constant.18.clone.tz_ref), custom_call_target="tpu_custom_call" | custom-call | tf_op jit(solution)/shard_map/template_spectrum/pallas_call | solution.py:520
  20.7 21.0 %correlate.1 = (f32[32,32,128]{2,1,0:T(8,128)}, f32[8,32,128]{2,1,0:T(8,128)}) custom-call(f32[32,80,128]{2,1,0:T(8,128)} %get-tuple-element.9.ext_ref, f32[40,72,256]{2,1,0:T(8,128)} %get-tuple-element.10.khat_hbm, f32[64,72,256]{2,1,0:T(8,128)} %constant.20.clone.mhat_hbm, f32[4,16]{1,0:T(4,128)} %constant.21.clone.phase_ref, ...), custom_call_target="tpu_custom_call" | custom-call | tf_op jit(solution)/shard_map/correlate/pallas_call | solution.py:541
  41.7 10.0 %exchange.1 = f32[8,32,128]{2,1,0:T(8,128)} custom-call(f32[32,32,128]{2,1,0:T(8,128)} %get-tuple-element.11.score_ref, f32[8,32,128]{2,1,0:T(8,128)} %get-tuple-element.12.scale_ref), custom_call_target="tpu_custom_call" | custom-call | tf_op jit(solution)/shard_map/exchange/pallas_call | solution.py:570
  51.7 1.6 %copy.13 = f32[1,8,32,128]{3,2,1,0:T(8,128)} copy(f32[1,8,32,128]{3,2,1,0:T(8,128)} %bitcast.7) | data formatting | bytes 262144

commit v3 on v2

--- a/solution.py
+++ b/solution.py
@@ -229,6 +229,16 @@
     def _():
         pl.semaphore_signal(barrier, inc=1, device_id={"tile": tile + 1}, device_id_type=pl.DeviceIdType.MESH)
 
+    pl.semaphore_wait(barrier, before.astype(jnp.int32) + after.astype(jnp.int32) + 1)
+
+    @pl.when(before)
+    def _():
+        to_previous().start()
+
+    @pl.when(after)
+    def _():
+        to_next().start()
+
     grid_ref[...] = jnp.zeros(grid_ref.shape, jnp.float32)
     grid_ref[:, :TMPL, :TMPL] = raw_ref[...].astype(jnp.float32)
     shape = grid_ref.shape[1:]
@@ -251,16 +261,6 @@
 
     squares = jnp.sum(lax.fori_loop(0, TMPL, add_square, zeros, unroll=4), keepdims=True)
     scale = 1.0 / jnp.sqrt(squares / voxels + EPSILON)
-
-    pl.semaphore_wait(barrier, before.astype(jnp.int32) + after.astype(jnp.int32) + 1)
-
-    @pl.when(before)
-    def _():
-        to_previous().start()
-
-    @pl.when(after)
-    def _():
-        to_next().start()
 
     ext_ref[:, rim : rim + size_y, :] = block_ref[...]
     nothing = jnp.zeros((block_ref.shape[0], rim, LANES), jnp.float32)
@@ -308,42 +308,11 @@
         to_mate(rim + size_y, 3).wait()
 
 
-def exchange_kernel(rots, score_ref, scale_ref, out_ref, others, send_sem, recv_sem):
-    me = lax.axis_index("rot")
-    rows = scale_ref.shape[0]
-    barrier = pltpu.get_barrier_semaphore()
-    peers = [lax.rem(me + d, rots) for d in range(1, rots)]
-    for peer in peers:
-        pl.semaphore_signal(barrier, inc=1, device_id={"rot": peer}, device_id_type=pl.DeviceIdType.MESH)
-    pl.semaphore_wait(barrier, rots - 1)
-    copies = []
-    for d, peer in enumerate(peers):
-        copy = pltpu.make_async_remote_copy(
-            src_ref=score_ref.at[pl.ds(peer * rows, rows)],
-            dst_ref=others.at[d],
-            send_sem=send_sem.at[d],
-            recv_sem=recv_sem.at[d],
-            device_id={"rot": peer},
-            device_id_type=pl.DeviceIdType.MESH,
-        )
-        copy.start()
-        copies.append(copy)
-    scale = scale_ref[...]
-    scores = [score_ref[pl.ds(me * rows, rows)] * scale]
-    for copy in copies:
-        copy.wait()
-    for d in range(rots - 1):
-        scores.append(others[d] * scale)
-    largest = functools.reduce(jnp.maximum, scores)
-    total = functools.reduce(jnp.add, [jnp.exp(score - largest) for score in scores])
-    out_ref[...] = largest + jnp.log(total)
-
-
 def main_kernel(
     dims, places, voxels,
     ext_ref, khat_hbm, mhat_hbm, phase_ref, ly_ref, tz_ref, iy_ref, iz_ref,
-    score_ref, scale_ref,
-    fields, khat_ref, mhat, stage, mixed, rows, local, sem,
+    largest_ref, total_ref,
+    fields, khat_ref, mhat, stage, mixed, rows, local, others, sem, send_sem, recv_sem,
 ):
     size_in, length_y, padded, size_x, size_y, inner, outer = dims
     length_x = inner * outer
@@ -354,6 +323,12 @@
     for fetch in fetches:
         fetch.start()
     me = lax.axis_index("rot")
+    rots = size_x // inner
+    mate = me + 1 - 2 * lax.rem(me, 2)
+    peers = (lax.rem(me + 2, rots), lax.rem(mate + 2, rots), mate)
+    barrier = pltpu.get_barrier_semaphore()
+    for peer in peers:
+        pl.semaphore_signal(barrier, inc=1, device_id={"rot": peer}, device_id_type=pl.DeviceIdType.MESH)
 
     def forward(step, carry):
         pairs = []
@@ -455,27 +430,43 @@
 
     lax.fori_loop(0, length_y // 8, block, 0)
 
-    group = 8
-
-    def inverse(step, carry):
+    def inverse(part):
         flat = []
-        for i in range(group):
-            o = dot(iy_ref[...], pieces(rows[step * group + i], 0))
+        for i in range(inner):
+            o = dot(iy_ref[...], pieces(rows[part * inner + i], 0))
             c, s = o[:size_y], o[size_y:]
             re = c[:, :LANES] - s[:, LANES:]
             im = c[:, LANES:] + s[:, :LANES]
             flat.append(jnp.concatenate([re, im], axis=1))
         result = dot(pieces(jnp.concatenate(flat, axis=0), 1), iz_ref[...])
-        for i in range(group):
-            local[step * group + i] = result[i * size_y : (i + 1) * size_y]
-        return carry
-
-    lax.fori_loop(0, (size_x + 2 * inner) // group, inverse, 0)
-    score_ref[...] = local[:size_x]
-    mean = local[size_x : size_x + inner] / voxels
-    square = local[size_x + inner :] / voxels
+        return result.reshape(inner, size_y, LANES)
+
+    pl.semaphore_wait(barrier, len(peers))
+    copies = []
+    for slot, peer in enumerate(peers):
+        local[slot] = inverse(peer)
+        copy = pltpu.make_async_remote_copy(
+            src_ref=local.at[slot],
+            dst_ref=others.at[slot],
+            send_sem=send_sem.at[slot],
+            recv_sem=recv_sem.at[slot],
+            device_id={"rot": peer},
+            device_id_type=pl.DeviceIdType.MESH,
+        )
+        copy.start()
+        copies.append(copy)
+    mean = inverse(rots) / voxels
+    square = inverse(rots + 1) / voxels
     std = jnp.sqrt(jnp.maximum(square - mean * mean, VAR_FLOOR))
-    scale_ref[...] = SHARPNESS / (math.sqrt(voxels) * std)
+    scale = SHARPNESS / (math.sqrt(voxels) * std)
+    scores = [inverse(me) * scale]
+    for copy in copies:
+        copy.wait()
+    for slot in range(len(peers)):
+        scores.append(others[slot] * scale)
+    largest = functools.reduce(jnp.maximum, scores)
+    largest_ref[...] = largest
+    total_ref[...] = functools.reduce(jnp.add, [jnp.exp(score - largest) for score in scores])
 
 
 def row_halo(block, across):
@@ -538,10 +529,10 @@
     turns = angles(outer, np.arange(rots), np.arange(outer))
     phase = jnp.asarray(np.stack([np.cos(turns), np.sin(turns)], axis=2).reshape(rots, 2 * outer).astype(np.float32))
     dims = (size_in, length_y, padded, size_x, size_y, inner, outer)
-    scores, scale = pl.pallas_call(
+    largest, total = pl.pallas_call(
         functools.partial(main_kernel, dims, places, voxels),
         out_shape=(
-            jax.ShapeDtypeStruct((size_x, size_y, size_z), jnp.float32),
+            jax.ShapeDtypeStruct((inner, size_y, size_z), jnp.float32),
             jax.ShapeDtypeStruct((inner, size_y, size_z), jnp.float32),
         ),
         in_specs=[
@@ -556,10 +547,13 @@
             pltpu.VMEM((3, length_x, 8, 2 * LANES), jnp.float32),
             pltpu.VMEM((3, length_x, 8, 2 * LANES), jnp.float32),
             pltpu.VMEM((size_x + 2 * inner, padded, 2 * LANES), jnp.float32),
-            pltpu.VMEM((size_x + 2 * inner, size_y, size_z), jnp.float32),
+            pltpu.VMEM((rots - 1, inner, size_y, size_z), jnp.float32),
+            pltpu.VMEM((rots - 1, inner, size_y, size_z), jnp.float32),
             pltpu.SemaphoreType.DMA((2,)),
+            pltpu.SemaphoreType.DMA((rots - 1,)),
+            pltpu.SemaphoreType.DMA((rots - 1,)),
         ],
-        compiler_params=pltpu.CompilerParams(vmem_limit_bytes=VMEM),
+        compiler_params=pltpu.CompilerParams(vmem_limit_bytes=VMEM, collective_id=1, has_side_effects=True),
         name="correlate",
     )(
         extended, khat, mhat, phase,
@@ -567,20 +561,7 @@
         jnp.asarray(y_inverse(length_y, padded, size_y)),
         jnp.asarray(z_inverse(length_z, size_z, freqs, length_x)),
     )
-    result = pl.pallas_call(
-        functools.partial(exchange_kernel, rots),
-        out_shape=jax.ShapeDtypeStruct((inner, size_y, size_z), jnp.float32),
-        in_specs=[vmem, vmem],
-        out_specs=vmem,
-        scratch_shapes=[
-            pltpu.VMEM((rots - 1, inner, size_y, size_z), jnp.float32),
-            pltpu.SemaphoreType.DMA((rots - 1,)),
-            pltpu.SemaphoreType.DMA((rots - 1,)),
-        ],
-        compiler_params=pltpu.CompilerParams(vmem_limit_bytes=VMEM, collective_id=1, has_side_effects=True),
-        name="exchange",
-    )(scores, scale)
-    return result[None]
+    return (largest + jnp.log(total))[None]
 
 
 def solution(mesh):

time: 53.5 us -> 48.9 us (0.914)
  Pallas kernels: 47.6 us -> 43 us
  other arithmetic: 0 us -> 1.65 us
  local copies, waits for them, and re-layouts: 4.94 us -> 3.37 us
    pallas_call x1 -> x0, Pallas kernels: 9.99 us -> none  [shards(): pl.pallas_call(functools.partial(exchange_kernel, rots), out_shape=jax.Sh...]
    pallas_call x1, Pallas kernels: 21 us -> 26.3 us  [shards(): pl.pallas_call(functools.partial(main_kernel, dims, places, voxels), out_...]
    broadcast_in_dim x0 -> x1, other arithmetic: none -> 1.65 us  [shards(): return (largest + jnp.log(total))[None]]
    unnamed x1 -> x0, local copies, waits for them, and re-layouts: 1.57 us -> none
where the time goes in v3:
time: 48.9 us; the launch traced here: 48.7 us
  Pallas kernels  43 us (88%)
  local copies, waits for them, and re-layouts  3.37 us (7%)
  other arithmetic  1.65 us (3%)
  between operations  0.68 us (1%)
    pallas_call x1, Pallas kernels, shards(): pl.pallas_call(functools.partial(main_kernel, dims, places, voxels), out_...  26.3 us
    pallas_call x1, Pallas kernels, shards(): pl.pallas_call(functools.partial(template_kernel, length_y, across, rim,...  16.6 us
    dynamic_slice x1, local copies, waits for them, and re-layouts, shards(): grid = templates[rot_ids[0]].reshape(TMPL, TMPL, TMPL)  2.01 us
    broadcast_in_dim x1, other arithmetic, shards(): return (largest + jnp.log(total))[None]  1.65 us
    another operation x1, local copies, waits for them, and re-layouts, shards(): grid = templates[rot_ids[0]].reshape(TMPL, TMPL, TMPL)  1.36 us

profile of v3, /device:TPU:9, one launch (start us, length us, event | category | flops | bytes accessed | tf_op | source)
XLA Modules:
  0.0 48.7 jit_solution(13991247562178473221)
XLA Ops:
  0.7 2.0 %dynamic-slice_reduce_fusion = bf16[64000]{0:T(1024)(128)(2,1)S(1)} fusion(bf16[32,64000]{1,0:T(8,128)(2,1)} %param.11, s32[]{:T(128)S(6)} %select_n.3), kind=kLoop, calls=%fused_computation | loop fusion | bytes 256004 | tf_op jit(solution)/shard_map/dynamic_slice | solution.py:509
  2.7 1.4 %reshape_squeeze.3.raw_ref = bf16[40,40,40]{2,1,0:T(8,128)(2,1)} reshape(bf16[64000]{0:T(1024)(128)(2,1)S(1)} %dynamic-slice_reduce_fusion) | data formatting | bytes 256000 | tf_op jit(solution)/shard_map/reshape;squeeze | solution.py:509
  4.0 16.6 %template_spectrum.1 = (f32[40,72,256]{2,1,0:T(8,128)}, f32[32,80,128]{2,1,0:T(8,128)}) custom-call(bf16[40,40,40]{2,1,0:T(8,128)(2,1)} %reshape_squeeze.3.raw_ref, f32[32,32,128]{2,1,0:T(8,128)} %bitcast.7, bf16[144,144]{1,0:T(8,128)(2,1)} %constant.19.clone.ly_ref, bf16[384,256]{1,0:T(8,128)(2,1)} %constant.18.clone.tz_ref), custom_call_target="tpu_custom_call" | custom-call | tf_op jit(solution)/shard_map/template_spectrum/pallas_call | solution.py:511
  20.7 26.3 %correlate.1 = (f32[8,32,128]{2,1,0:T(8,128)}, f32[8,32,128]{2,1,0:T(8,128)}) custom-call(f32[32,80,128]{2,1,0:T(8,128)} %get-tuple-element.9.ext_ref, f32[40,72,256]{2,1,0:T(8,128)} %get-tuple-element.10.khat_hbm, f32[64,72,256]{2,1,0:T(8,128)} %constant.20.clone.mhat_hbm, f32[4,16]{1,0:T(4,128)} %constant.21.clone.phase_ref, ...), custom_call_target="tpu_custom_call" | custom-call | tf_op jit(solution)/shard_map/correlate/pallas_call | solution.py:532
  47.0 1.6 %add_bitcast_fusion = f32[1,8,32,128]{3,2,1,0:T(8,128)} fusion(f32[8,32,128]{2,1,0:T(8,128)} %get-tuple-element.11, f32[8,32,128]{2,1,0:T(8,128)} %get-tuple-element.12), kind=kLoop, calls=%fused_computation.1 | loop fusion | flops 32768 | bytes 393216 | tf_op jit(solution)/shard_map/broadcast_in_dim | solution.py:564

commit v4 on v3

--- a/solution.py
+++ b/solution.py
@@ -175,9 +175,9 @@
     return outs
 
 
-def template_kernel(
+def halo_and_template(
     length_y, across, rim, voxels, raw_ref, block_ref, ly_ref, tz_ref, out_ref, ext_ref,
-    grid_ref, send_sem, recv_sem,
+    grid_ref, send_sem, recv_sem, peers,
 ):
     tile = lax.axis_index("tile")
     core = lax.rem(lax.axis_index("rot"), 2)
@@ -219,7 +219,8 @@
             device_id_type=pl.DeviceIdType.MESH,
         )
 
-    pl.semaphore_signal(barrier, inc=1, device_id={"rot": mate}, device_id_type=pl.DeviceIdType.MESH)
+    for peer in peers:
+        pl.semaphore_signal(barrier, inc=1, device_id={"rot": peer}, device_id_type=pl.DeviceIdType.MESH)
 
     @pl.when(before)
     def _():
@@ -229,7 +230,7 @@
     def _():
         pl.semaphore_signal(barrier, inc=1, device_id={"tile": tile + 1}, device_id_type=pl.DeviceIdType.MESH)
 
-    pl.semaphore_wait(barrier, before.astype(jnp.int32) + after.astype(jnp.int32) + 1)
+    pl.semaphore_wait(barrier, before.astype(jnp.int32) + after.astype(jnp.int32) + len(peers))
 
     @pl.when(before)
     def _():
@@ -310,25 +311,23 @@
 
 def main_kernel(
     dims, places, voxels,
-    ext_ref, khat_hbm, mhat_hbm, phase_ref, ly_ref, tz_ref, iy_ref, iz_ref,
+    raw_ref, block_ref, mhat_hbm, phase_ref, lk_ref, ly_ref, tz_ref, iy_ref, iz_ref,
     largest_ref, total_ref,
-    fields, khat_ref, mhat, stage, mixed, rows, local, others, sem, send_sem, recv_sem,
+    grid_ref, ext_ref, fields, khat_ref, mhat, stage, mixed, rows, local, others,
+    sem, rim_send, rim_recv, send_sem, recv_sem,
 ):
-    size_in, length_y, padded, size_x, size_y, inner, outer = dims
+    size_in, length_y, padded, size_x, size_y, inner, outer, across, rim = dims
     length_x = inner * outer
-    fetches = [
-        pltpu.make_async_copy(khat_hbm, khat_ref, sem.at[0]),
-        pltpu.make_async_copy(mhat_hbm, mhat, sem.at[1]),
-    ]
-    for fetch in fetches:
-        fetch.start()
+    fetch = pltpu.make_async_copy(mhat_hbm, mhat, sem)
+    fetch.start()
     me = lax.axis_index("rot")
     rots = size_x // inner
     mate = me + 1 - 2 * lax.rem(me, 2)
     peers = (lax.rem(me + 2, rots), lax.rem(mate + 2, rots), mate)
-    barrier = pltpu.get_barrier_semaphore()
-    for peer in peers:
-        pl.semaphore_signal(barrier, inc=1, device_id={"rot": peer}, device_id_type=pl.DeviceIdType.MESH)
+    halo_and_template(
+        length_y, across, rim, voxels, raw_ref, block_ref, lk_ref, tz_ref, khat_ref, ext_ref,
+        grid_ref, rim_send, rim_recv, peers,
+    )
 
     def forward(step, carry):
         pairs = []
@@ -342,8 +341,7 @@
 
     lax.fori_loop(0, size_in // 4, forward, 0)
     rows[:, length_y:, :] = jnp.zeros((rows.shape[0], padded - length_y, 2 * LANES), jnp.float32)
-    for fetch in fetches:
-        fetch.wait()
+    fetch.wait()
 
     def block(r, carry):
         at = pl.ds(pl.multiple_of(r * 8, 8), 8)
@@ -441,7 +439,6 @@
         result = dot(pieces(jnp.concatenate(flat, axis=0), 1), iz_ref[...])
         return result.reshape(inner, size_y, LANES)
 
-    pl.semaphore_wait(barrier, len(peers))
     copies = []
     for slot, peer in enumerate(peers):
         local[slot] = inverse(peer)
@@ -508,27 +505,10 @@
     kernel_rows = 48
     grid = templates[rot_ids[0]].reshape(TMPL, TMPL, TMPL)
     vmem = pl.BlockSpec(memory_space=pltpu.VMEM)
-    khat, extended = pl.pallas_call(
-        functools.partial(template_kernel, length_y, across, rim, voxels),
-        out_shape=(
-            jax.ShapeDtypeStruct((TMPL, length_y, 2 * LANES), jnp.float32),
-            jax.ShapeDtypeStruct((size_in, reach, size_z), jnp.float32),
-        ),
-        in_specs=[vmem] * 4,
-        out_specs=(vmem, vmem),
-        scratch_shapes=[
-            pltpu.VMEM((TMPL, kernel_rows, LANES), jnp.float32),
-            pltpu.SemaphoreType.DMA((4,)),
-            pltpu.SemaphoreType.DMA((4,)),
-        ],
-        compiler_params=pltpu.CompilerParams(vmem_limit_bytes=VMEM, collective_id=0, has_side_effects=True),
-        name="template_spectrum",
-    )(grid, block, jnp.asarray(y_forward(length_y, kernel_rows, 0)), tz)
-
     mhat = jnp.asarray(mask_spectrum(places, length_x, length_y, length_z, freqs))
     turns = angles(outer, np.arange(rots), np.arange(outer))
     phase = jnp.asarray(np.stack([np.cos(turns), np.sin(turns)], axis=2).reshape(rots, 2 * outer).astype(np.float32))
-    dims = (size_in, length_y, padded, size_x, size_y, inner, outer)
+    dims = (size_in, length_y, padded, size_x, size_y, inner, outer, across, rim)
     largest, total = pl.pallas_call(
         functools.partial(main_kernel, dims, places, voxels),
         out_shape=(
@@ -536,11 +516,13 @@
             jax.ShapeDtypeStruct((inner, size_y, size_z), jnp.float32),
         ),
         in_specs=[
-            vmem, pl.BlockSpec(memory_space=pl.ANY), pl.BlockSpec(memory_space=pl.ANY), pl.BlockSpec(memory_space=pltpu.SMEM),
-            vmem, vmem, vmem, vmem,
+            vmem, vmem, pl.BlockSpec(memory_space=pl.ANY), pl.BlockSpec(memory_space=pltpu.SMEM),
+            vmem, vmem, vmem, vmem, vmem,
         ],
         out_specs=(vmem, vmem),
         scratch_shapes=[
+            pltpu.VMEM((TMPL, kernel_rows, LANES), jnp.float32),
+            pltpu.VMEM((size_in, reach, size_z), jnp.float32),
             pltpu.VMEM((2, size_in, length_y, 2 * LANES), jnp.float32),
             pltpu.VMEM((TMPL, length_y, 2 * LANES), jnp.float32),
             pltpu.VMEM((length_x, length_y, 2 * LANES), jnp.float32),
@@ -549,14 +531,17 @@
             pltpu.VMEM((size_x + 2 * inner, padded, 2 * LANES), jnp.float32),
             pltpu.VMEM((rots - 1, inner, size_y, size_z), jnp.float32),
             pltpu.VMEM((rots - 1, inner, size_y, size_z), jnp.float32),
-            pltpu.SemaphoreType.DMA((2,)),
+            pltpu.SemaphoreType.DMA,
+            pltpu.SemaphoreType.DMA((4,)),
+            pltpu.SemaphoreType.DMA((4,)),
             pltpu.SemaphoreType.DMA((rots - 1,)),
             pltpu.SemaphoreType.DMA((rots - 1,)),
         ],
-        compiler_params=pltpu.CompilerParams(vmem_limit_bytes=VMEM, collective_id=1, has_side_effects=True),
+        compiler_params=pltpu.CompilerParams(vmem_limit_bytes=VMEM, collective_id=0, has_side_effects=True),
         name="correlate",
     )(
-        extended, khat, mhat, phase,
+        grid, block, mhat, phase,
+        jnp.asarray(y_forward(length_y, kernel_rows, 0)),
         jnp.asarray(y_forward(length_y, reach, rim - HALF)), tz,
         jnp.asarray(y_inverse(length_y, padded, size_y)),
         jnp.asarray(z_inverse(length_z, size_z, freqs, length_x)),

time: 48.9 us -> 45.5 us (0.930)
  Pallas kernels: 43 us -> 39.6 us
    pallas_call x1 -> x0, Pallas kernels: 16.6 us -> none  [shards(): pl.pallas_call(functools.partial(template_kernel, length_y, across, rim,...]
    pallas_call x1, Pallas kernels: 26.3 us -> 39.6 us  [shards(): pl.pallas_call(functools.partial(main_kernel, dims, places, voxels), out_...]
where the time goes in v4:
time: 45.5 us; the launch traced here: 45.3 us
  Pallas kernels  39.6 us (87%)
  local copies, waits for them, and re-layouts  3.36 us (7%)
  other arithmetic  1.65 us (4%)
  between operations  0.67 us (1%)
    pallas_call x1, Pallas kernels, shards(): pl.pallas_call(functools.partial(main_kernel, dims, places, voxels), out_...  39.6 us
    dynamic_slice x1, local copies, waits for them, and re-layouts, shards(): grid = templates[rot_ids[0]].reshape(TMPL, TMPL, TMPL)  2.01 us
    broadcast_in_dim x1, other arithmetic, shards(): return (largest + jnp.log(total))[None]  1.65 us
    another operation x1, local copies, waits for them, and re-layouts, shards(): grid = templates[rot_ids[0]].reshape(TMPL, TMPL, TMPL)  1.35 us

profile of v4, /device:TPU:9, one launch (start us, length us, event | category | flops | bytes accessed | tf_op | source)
XLA Modules:
  0.0 45.3 jit_solution(1593312776052919999)
XLA Ops:
  0.7 2.0 %dynamic-slice_reduce_fusion = bf16[64000]{0:T(1024)(128)(2,1)S(1)} fusion(bf16[32,64000]{1,0:T(8,128)(2,1)} %param.11, s32[]{:T(128)S(6)} %select_n.3), kind=kLoop, calls=%fused_computation | loop fusion | bytes 256004 | tf_op jit(solution)/shard_map/dynamic_slice | solution.py:506
  2.7 1.4 %reshape_squeeze.3.raw_ref = bf16[40,40,40]{2,1,0:T(8,128)(2,1)} reshape(bf16[64000]{0:T(1024)(128)(2,1)S(1)} %dynamic-slice_reduce_fusion) | data formatting | bytes 256000 | tf_op jit(solution)/shard_map/reshape;squeeze | solution.py:506
  4.0 39.6 %correlate.1 = (f32[8,32,128]{2,1,0:T(8,128)}, f32[8,32,128]{2,1,0:T(8,128)}) custom-call(bf16[40,40,40]{2,1,0:T(8,128)(2,1)} %reshape_squeeze.3.raw_ref, f32[32,32,128]{2,1,0:T(8,128)} %bitcast.7, f32[64,72,256]{2,1,0:T(8,128)} %constant.19.clone.mhat_hbm, f32[4,16]{1,0:T(4,128)} %constant.20.clone.phase_ref, bf16[144,144]{1,0:T(8,128)(2,1)} %constant.21.clone.lk_ref, ...), custom_call_target="tpu_custom_call" | custom-call | tf_op jit(solution)/shard_map/correlate/pallas_call | solution.py:512
  43.7 1.6 %add_bitcast_fusion = f32[1,8,32,128]{3,2,1,0:T(8,128)} fusion(f32[8,32,128]{2,1,0:T(8,128)} %get-tuple-element.7, f32[8,32,128]{2,1,0:T(8,128)} %get-tuple-element.8), kind=kLoop, calls=%fused_computation.1 | loop fusion | flops 32768 | bytes 393216 | tf_op jit(solution)/shard_map/broadcast_in_dim | solution.py:549
